TPU v7x, 32 devices: a whole 2x2x4 slice. The times are simulated.
32 devices in a mesh: dp: 4 (over y, core), seq: 2 (over x), tensor: 4 (over z).
Axes of the slice: x: 2, y: 2, z: 4, core: 2. Of those that a mesh axis runs over, the one named last changes fastest.
Arguments:
- queries: bfloat16 [16384, 8192], P(('dp', 'seq'), 'tensor'), parts along dimension 0, may hold values from -110 to 110
- keys_values: bfloat16 [16384, 2, 1024], P(('dp', 'seq'), None, 'tensor'), parts along dimension 0, may hold values from -4.5 to 4.5
- out_weight: bfloat16 [8192, 8192], P('tensor', 'seq'), may hold values from -0.1875 to 0.1875
- residual: bfloat16 [16384, 8192], P(('dp', 'tensor'), 'seq'), parts along dimension 0, may hold values from -3 to 3
- segments: int32 [16384], P('dp'), parts along dimension 0, may hold values from 0 to 3, never falling along the last dimension, each value on 1 to 2048 neighbouring positions
Outputs:
- layer_out: bfloat16 [16384, 8192], P(('dp', 'tensor'), 'seq'), parts along dimension 0
There are 4 independent parts, one for each index of `dp`. A program takes and returns all parts, laid end to end along the dimension named above; an argument that names none is the same for every part. Nothing has to cross between parts.
Inputs may be any that keep to these rules, and one draw needn't show every extreme that they name: `segments`: segment numbers never fall along the tokens.
All inputs are finite; a program needn't handle non-finite values.
Results may differ from a plain program's by a relative error of at most 0.0085.
Values may be sent and summed in bfloat16 or wider, within the bound.
A program may use at most 384 MiB of HBM per device.

v0:
```python
import jax
import jax.numpy as jnp
import numpy as np
from jax import lax
from jax.sharding import PartitionSpec as P

H = 64
KVH = 8
HD = 128
L = 4096


def attend(query_all, pair_all, segments, heads_dev, kv_dev, group_size):
    all_rows = query_all.shape[0]
    seq_count = all_rows // L
    block_rows = min(512, L)
    head_map = np.array([member // group_size for member in range(heads_dev)], dtype=np.int32)
    query_four = query_all.reshape(seq_count, L, heads_dev, HD)
    key_heads = pair_all[:, 0, :].reshape(seq_count, L, kv_dev, HD)[:, :, head_map, :]
    value_heads = pair_all[:, 1, :].reshape(seq_count, L, kv_dev, HD)[:, :, head_map, :]
    doc_ids = segments.reshape(seq_count, L)
    score_scale = HD ** (-0.5)
    outputs = []
    for block_index in range(L // block_rows):
        first_row = block_index * block_rows
        key_end = first_row + block_rows
        query_block = query_four[:, first_row:key_end]
        raw_scores = (
            jnp.einsum(
                "sqhd,skhd->shqk",
                query_block,
                key_heads[:, :key_end],
                preferred_element_type=jnp.float32,
            )
            * score_scale
        )
        query_pos = first_row + jnp.arange(block_rows)[:, None]
        key_pos = jnp.arange(key_end)[None, :]
        same_doc = doc_ids[:, first_row:key_end, None] == doc_ids[:, None, :key_end]
        allowed = (key_pos <= query_pos)[None, None, :, :] & same_doc[:, None, :, :]
        masked = jnp.where(allowed, raw_scores, -1e30)
        highest = jnp.max(masked, axis=-1, keepdims=True)
        exponents = jnp.where(allowed, jnp.exp(masked - highest), 0.0)
        weights = (exponents / jnp.sum(exponents, axis=-1, keepdims=True)).astype(jnp.bfloat16)
        blended = jnp.einsum(
            "shqk,skhd->sqhd", weights, value_heads[:, :key_end], preferred_element_type=jnp.float32
        )
        outputs.append(blended.astype(jnp.bfloat16))
    return jnp.concatenate(outputs, axis=1).reshape(all_rows, heads_dev * HD)


def on_device(queries, keys_values, out_weight, residual, segments):
    n_seq = lax.axis_size("seq")
    tok_dev = queries.shape[0]
    heads_ten = queries.shape[1] // HD
    heads_dev = heads_ten // n_seq
    kv_ten = keys_values.shape[2] // HD
    group_size = H // KVH
    kv_dev = max(1, heads_dev // group_size)
    table = np.array(
        [
            target * heads_dev // group_size + member
            for target in range(n_seq)
            for member in range(kv_dev)
        ],
        dtype=np.int32,
    )
    picked = keys_values.reshape(tok_dev, 2, kv_ten, HD)[:, :, table, :].reshape(
        tok_dev, 2, n_seq * kv_dev * HD
    )
    query_slab = queries.reshape(tok_dev, 1, heads_ten * HD)
    query_all, pair_all = (
        lax.all_to_all(query_slab, "seq", split_axis=2, concat_axis=0, tiled=True),
        lax.all_to_all(picked, "seq", split_axis=2, concat_axis=0, tiled=True),
    )
    query_all = query_all.reshape(query_all.shape[0], heads_dev * HD)
    heads_out = attend(query_all, pair_all, segments, heads_dev, kv_dev, group_size)
    gathered = lax.all_gather(heads_out, "seq", axis=1, tiled=True)
    summed = lax.psum_scatter(
        jnp.dot(gathered, out_weight, preferred_element_type=jnp.float32),
        "tensor",
        scatter_dimension=0,
        tiled=True,
    )
    return (residual.astype(jnp.float32) + summed).astype(jnp.bfloat16)


def solution(mesh):
    placed = (
        P(("dp", "seq"), "tensor"),
        P(("dp", "seq"), None, "tensor"),
        P("tensor", "seq"),
        P(("dp", "tensor"), "seq"),
        P("dp"),
    )
    return jax.shard_map(
        on_device, mesh=mesh, in_specs=placed, out_specs=P(("dp", "tensor"), "seq"), check_vma=False
    )
```

profile of v0, /device:TPU:19, one launch (start us, length us, event | category | flops | bytes accessed | tf_op | source)
XLA Modules:
  0.0 1992.4 jit_solution(11687069901031470855)
XLA Ops:
  26.3 40.1 %copy.149 = bf16[2048,1,2048]{0,1,2:T(2,128)(2,1)} copy(bf16[2048,1,2048]{2,0,1:T(8,128)(2,1)} %bitcast.294) | data formatting | bytes 16777216 | tf_op jit(solution)/shard_map/reshape | solution.py:71
  67.0 51.2 %reduce.38 = bf16[2048,2048]{1,0:T(8,128)(2,1)} reduce(bf16[2048,1,2048]{2,1,0:T(2,128)(2,1)} %bitcast.282, bf16[]{:T(256)} %broadcast.646), dimensions={1}, to_apply=%bitcast.239.reduce_sub_computation | reduce | bytes 16777218
  118.1 10.2 reshape.896
  171.4 70.2 %all-to-all-done.1 = bf16[2,2,1048576]{2,1,0:T(2,128)(2,1)} async-done(((bf16[2,2,1048576]{2,1,0:T(2,128)(2,1)}), bf16[2,2,1048576]{2,1,0:T(2,128)(2,1)}, u32[]{:S(2)}, u32[]{:S(2)}) %all-to-all-start.1) | async-done | bytes 8388640 | tf_op jit(solution)/shard_map/all_to_all | solution.py:73
  241.6 17.8 reshape.897
  259.4 13.5 copy.182
  272.9 11.8 copy.150
  306.8 17.0 fusion.245
  329.0 11.6 fusion.237
  340.6 15.7 fusion.242
  364.5 11.4 fusion.193
  376.0 19.5 fusion.181
  395.5 24.2 %fusion.250 = (f32[8,512]{1,0:T(8,128)S(1)}, f32[8,512,2560]{1,2,0:T(8,128)}) fusion(pred[512,2560]{0,1:T(8,128)(4,1)S(1)} %copy-done.2, bf16[2560,128]{1,0:T(8,128)(2,1)S(1)} %copy-done.7, bf16[1,512,8,128]{3,2,1,0:T(8,128)(2,1)} %get-tuple-element.8), kind=kOutput, calls=%fused_computation.212 | convolution fusion | flops 2736785920 | bytes 44974080 | tf_op jit(solution)/shard_map/sub | solution.py:43
  419.7 29.3 %fusion.253 = (f32[8,512]{1,0:T(8,128)}, f32[8,512,3072]{1,2,0:T(8,128)}) fusion(pred[512,3072]{0,1:T(8,128)(4,1)S(1)} %copy-done.1, bf16[3072,128]{1,0:T(8,128)(2,1)} %get-tuple-element.18, bf16[1,512,8,128]{3,2,1,0:T(8,128)(2,1)} %get-tuple-element.7), kind=kOutput, calls=%fused_computation.213 | convolution fusion | flops 3284143104 | bytes 53755904 | tf_op jit(solution)/shard_map/sub | solution.py:43
  449.0 32.2 %fusion.258 = (f32[8,512]{1,0:T(8,128)}, f32[8,512,3584]{1,2,0:T(8,128)}) fusion(pred[512,3584]{0,1:T(8,128)(4,1)} %fusion.44, bf16[3584,128]{1,0:T(8,128)(2,1)} %get-tuple-element.16, bf16[1,512,8,128]{3,2,1,0:T(8,128)(2,1)} %get-tuple-element.6), kind=kOutput, calls=%fused_computation.214 | convolution fusion | flops 3831500288 | bytes 62537728 | tf_op jit(solution)/shard_map/sub | solution.py:43
  481.2 38.2 %fusion.261 = (f32[8,512]{1,0:T(8,128)}, f32[8,512,4096]{1,2,0:T(8,128)}) fusion(pred[512,4096]{0,1:T(8,128)(4,1)S(1)} %copy-done, bf16[4096,128]{1,0:T(8,128)(2,1)} %get-tuple-element.14, bf16[1,512,8,128]{3,2,1,0:T(8,128)(2,1)S(1)} %copy-done.3), kind=kOutput, calls=%fused_computation.215 | convolution fusion | flops 4378857472 | bytes 71319552 | tf_op jit(solution)/shard_map/sub | solution.py:43
  519.4 15.8 fusion.169
  535.2 18.3 fusion.163
  553.5 20.6 %fusion.157 = bf16[1,4096,8,128]{1,3,2,0:T(8,128)(2,1)} fusion(bf16[1,4096,8,128]{1,3,2,0:T(8,128)(2,1)} %fusion.163, f32[8,512,3584]{1,2,0:T(8,128)} %get-tuple-element.48, f32[8,512]{1,0:T(8,128)S(1)} %copy-done.14, bf16[3584,128]{0,1:T(8,128)(2,1)S(1)} %copy-done.5), kind=kOutput, calls=%fused_computation.132 | convolution fusion | flops 3787980800 | bytes 60702720 | tf_op jit(solution)/shard_map/shqk,skhd->sqhd/dot_general | solution.py:45
  574.0 22.9 %fusion.151 = bf16[1,4096,8,128]{1,3,2,0:T(8,128)(2,1)} fusion(bf16[1,4096,8,128]{1,3,2,0:T(8,128)(2,1)} %fusion.157, f32[8,512,4096]{1,2,0:T(8,128)} %get-tuple-element.50, f32[8,512]{1,0:T(8,128)S(1)} %copy-done.17, bf16[4096,128]{0,1:T(8,128)(2,1)S(1)} %copy-done.4), kind=kOutput, calls=%fused_computation.130 | convolution fusion | flops 4329046016 | bytes 69222400 | tf_op jit(solution)/shard_map/shqk,skhd->sqhd/dot_general | solution.py:45
  597.0 200.0 %all-gather.2.cloned.1.call-done = bf16[4096,2048]{0,1:T(8,128)(2,1)} async-done(((bf16[4096,1024]{0,1:T(8,128)(2,1)}), bf16[4096,2048]{0,1:T(8,128)(2,1)}) %all-gather.2.cloned.1.call-update) | async-done | bytes 16777232 | tf_op jit(solution)/shard_map/all_gather | solution.py:78
  796.9 79.6 %fusion.266 = f32[4096,4096]{1,0:T(8,128)} fusion(bf16[4096,2048]{0,1:T(8,128)(2,1)} %all-gather.2.cloned.1.call-done, bf16[2048,4096]{1,0:T(8,128)(2,1)} %param.12), kind=kOutput, calls=%fused_computation.216 | convolution fusion | flops 68719476736 | bytes 100663296 | tf_op jit(solution)/shard_map/dot_general | solution.py:80
  876.6 1096.5 %reduce-scatter.4.cloned.1.call-done = f32[1024,4096]{1,0:T(8,128)} async-done(((f32[4096,4096]{1,0:T(8,128)}), f32[1024,4096]{1,0:T(8,128)}) %reduce-scatter.4.cloned.1.call-update) | async-done | bytes 16777232
  1973.1 12.0 add_convert_fusion
  (97 shorter events, 98.8 us)
Async XLA Ops:
  14.4 11.5 copy-start.9
  21.7 121.9 %all-to-all-start = ((bf16[2048,2,256]{0,1,2:T(2,128)(2,1)}), bf16[2048,2,256]{0,1,2:T(2,128)(2,1)S(1)}, u32[]{:S(2)}, u32[]{:S(2)}) async-start(bf16[2048,2,256]{0,1,2:T(2,128)(2,1)} %copy.145), calls=%async_computation | async-start | bytes 4194304 | tf_op jit(solution)/shard_map/all_to_all | solution.py:74
  143.6 98.0 %all-to-all-start.1 = ((bf16[2,2,1048576]{2,1,0:T(2,128)(2,1)}), bf16[2,2,1048576]{2,1,0:T(2,128)(2,1)}, u32[]{:S(2)}, u32[]{:S(2)}) async-start(bf16[2,2,1048576]{2,1,0:T(2,128)(2,1)} %reshape.896), calls=%async_computation.1 | async-start | bytes 16777216 | tf_op jit(solution)/shard_map/all_to_all | solution.py:73
  151.0 645.9 %all-gather.2.cloned.1.call-start = ((), (), s32[]{:S(2)}) async-start(), calls=%async_computation.3 | async-start | bytes 25165824 | tf_op jit(solution)/shard_map/all_gather | solution.py:78
  306.8 17.0 copy-start.13
  329.0 11.6 copy-start.11
  340.6 15.8 copy-start.12
  356.4 8.2 copy-start.10
  364.5 11.4 copy-start.8
  364.5 11.4 copy-start.15
  376.0 19.5 copy-start.2
  376.0 19.5 copy-start.7
  395.5 24.2 %copy-start.1 = (pred[512,3072]{0,1:T(8,128)(4,1)S(1)}, pred[512,3072]{0,1:T(8,128)(4,1)}, u32[]{:S(2)}) copy-start(pred[512,3072]{0,1:T(8,128)(4,1)} %fusion.50) | copy-start | bytes 4718596
  449.0 32.2 %copy-start = (pred[512,4096]{0,1:T(8,128)(4,1)S(1)}, pred[512,4096]{0,1:T(8,128)(4,1)}, u32[]{:S(2)}) copy-start(pred[512,4096]{0,1:T(8,128)(4,1)} %fusion.41) | copy-start | bytes 6291460
  449.0 32.2 %copy-start.3 = (bf16[1,512,8,128]{3,2,1,0:T(8,128)(2,1)S(1)}, bf16[1,512,8,128]{3,2,1,0:T(8,128)(2,1)}, u32[]{:S(2)}) copy-start(bf16[1,512,8,128]{3,2,1,0:T(8,128)(2,1)} %get-tuple-element.5) | copy-start | bytes 3145732
  519.4 15.8 copy-start.6
  519.4 15.8 copy-start.16
  535.2 18.3 copy-start.5
  535.2 18.3 copy-start.14
  553.5 20.6 %copy-start.4 = (bf16[4096,128]{0,1:T(8,128)(2,1)S(1)}, bf16[4096,128]{0,1:T(8,128)(2,1)}, u32[]{:S(2)}) copy-start(bf16[4096,128]{0,1:T(8,128)(2,1)} %copy.171) | copy-start | bytes 3145732
  553.5 20.6 %copy-start.17 = (f32[8,512]{1,0:T(8,128)S(1)}, f32[8,512]{1,0:T(8,128)}, u32[]{:S(2)}) copy-start(f32[8,512]{1,0:T(8,128)} %get-tuple-element.49) | copy-start | bytes 49156
  596.9 1376.2 %reduce-scatter.4.cloned.1.call-start = ((), (), s32[]{:S(2)}) async-start(), calls=%async_computation.4 | async-start | bytes 83886080
Sparse Core Ops, SparseCore 0:
  597.1 199.8 all-gather.1
  876.7 1096.3 reduce-scatter.3
where the time goes:
time: 2000 us; the launch traced here: 1990 us
  waiting for transfers between devices  1370 us (68%)
  matrix products  371 us (19%)
  local copies, waits for them, and re-layouts  144 us (7%)
  other arithmetic  84.9 us (4%)
    unnamed x3, waiting for transfers between devices  1100 us
    all_gather x1, waiting for transfers between devices, on_device(): gathered = lax.all_gather(heads_out, 'seq', axis=1, tiled=True)  200 us
    sub x7, matrix products, attend(): exponents = jnp.where(allowed, jnp.exp(masked - highest), 0.0)  168 us
    dot_general x8, matrix products, attend(): jnp.einsum('shqk,skhd->sqhd', weights, value_heads[:, :key_end], preferre...  122 us
    dot_general x1, matrix products, on_device(): jnp.dot(gathered, out_weight, preferred_element_type=jnp.float32)  79.6 us
    all_to_all x1, waiting for transfers between devices, on_device(): lax.all_to_all(query_slab, 'seq', split_axis=2, concat_axis=0, tiled=True)  70.2 us
    unnamed x42, local copies, waits for them, and re-layouts  57.1 us
    unnamed x1, other arithmetic  51.2 us
  transfers between devices with their start and end apart: 4, of which 3 were waited for; matrix products, arithmetic and copies ran while one was open for 7% of the time, Pallas kernels for 0%

commit v1 on v0

v1 whole, which is shorter than its diff:
```python
import functools

import jax
import jax.numpy as jnp
from jax import lax
from jax.experimental import pallas as pl
from jax.experimental.pallas import tpu as pltpu
from jax.sharding import PartitionSpec as P

H = 64
KVH = 8
HD = 128
L = 4096
NEG = -1e30
LOG2E = 1.4426950408889634


def attend_kernel(block, heads, starts_ref, q_ref, k_ref, vt_ref, first_ref, o_ref, m_ref, l_ref, acc_ref):
    at = pl.program_id(1)
    row0 = at * block
    low = starts_ref[2 * at] // block
    mid_low = jnp.minimum((starts_ref[2 * at + 1] + block - 1) // block, at)
    mid_low = jnp.maximum(mid_low, low)
    m_ref[...] = jnp.full(m_ref.shape, NEG, jnp.float32)
    l_ref[...] = jnp.zeros(l_ref.shape, jnp.float32)
    acc_ref[...] = jnp.zeros(acc_ref.shape, jnp.float32)
    scale = HD ** (-0.5) * LOG2E

    def step(masked, kb, carry):
        key0 = pl.multiple_of(kb * block, block)
        keys = k_ref[pl.ds(key0, block), :]
        values_t = vt_ref[:, pl.ds(key0, block)]
        if masked:
            key_pos = key0 + lax.broadcasted_iota(jnp.int32, (block, block), 0)
            query_pos = row0 + lax.broadcasted_iota(jnp.int32, (block, block), 1)
            allowed = (key_pos <= query_pos) & (key_pos >= first_ref[0:1, :])
        for head in range(heads):
            s = lax.dot_general(
                keys,
                q_ref[:, head * HD : (head + 1) * HD],
                (((1,), (1,)), ((), ())),
                preferred_element_type=jnp.float32,
            )
            s = s * scale
            if masked:
                s = jnp.where(allowed, s, NEG)
            m_old = m_ref[head : head + 1, :]
            m_new = jnp.maximum(m_old, jnp.max(s, axis=0, keepdims=True))
            alpha = jnp.exp2(m_old - m_new)
            p = jnp.exp2(s - m_new)
            l_ref[head : head + 1, :] = alpha * l_ref[head : head + 1, :] + jnp.sum(p, axis=0, keepdims=True)
            m_ref[head : head + 1, :] = m_new
            acc_ref[head] = alpha * acc_ref[head] + jnp.dot(
                values_t, p.astype(jnp.bfloat16), preferred_element_type=jnp.float32
            )
        return carry

    lax.fori_loop(low, mid_low, functools.partial(step, True), 0)
    lax.fori_loop(mid_low, at, functools.partial(step, False), 0)
    step(True, at, 0)
    for head in range(heads):
        blended = acc_ref[head] / l_ref[head : head + 1, :]
        o_ref[:, head * HD : (head + 1) * HD] = blended.T.astype(o_ref.dtype)


def attend(starts, query, keys, values_t, first, head0, count, group_size):
    rows = query.shape[0]
    block = 512
    heads = min(2, count)
    blocks = rows // block
    grid_spec = pltpu.PrefetchScalarGridSpec(
        num_scalar_prefetch=1,
        grid=(count // heads, blocks),
        in_specs=[
            pl.BlockSpec((block, heads * HD), lambda h, b, s: (b, head0 // heads + h)),
            pl.BlockSpec((rows, HD), lambda h, b, s: (0, (head0 + h * heads) // group_size)),
            pl.BlockSpec((HD, rows), lambda h, b, s: ((head0 + h * heads) // group_size, 0)),
            pl.BlockSpec((8, block), lambda h, b, s: (0, b)),
        ],
        out_specs=pl.BlockSpec((block, heads * HD), lambda h, b, s: (b, h)),
        scratch_shapes=[
            pltpu.VMEM((8, block), jnp.float32),
            pltpu.VMEM((8, block), jnp.float32),
            pltpu.VMEM((heads, HD, block), jnp.float32),
        ],
    )
    return pl.pallas_call(
        functools.partial(attend_kernel, block, heads),
        grid_spec=grid_spec,
        out_shape=jax.ShapeDtypeStruct((rows, count * HD), jnp.bfloat16),
        compiler_params=pltpu.CompilerParams(vmem_limit_bytes=32 * 1024 * 1024),
        cost_estimate=pl.CostEstimate(
            flops=4 * count * rows * rows * HD,
            bytes_accessed=4 * count * rows * HD,
            transcendentals=count * rows * rows // 2,
        ),
    )(starts, query, keys, values_t, first)


def shift(array, axis, by):
    size = lax.axis_size(axis)
    return lax.ppermute(array, axis, [(i, (i + by) % size) for i in range(size)])


def gather_weight(out_weight):
    n_dp, n_ten = lax.axis_size("dp"), lax.axis_size("tensor")
    dp, ten = lax.axis_index("dp"), lax.axis_index("tensor")
    rows, columns = out_weight.shape
    part = rows // n_dp
    half = part // 2
    forward = lax.dynamic_slice(out_weight, (dp * part, 0), (half, columns))
    back = lax.dynamic_slice(out_weight, (dp * part + half, 0), (half, columns))
    full = jnp.zeros((rows * n_ten, columns), out_weight.dtype)
    full = lax.dynamic_update_slice(full, out_weight, (ten * rows, 0))
    for k in range(1, n_ten):
        forward = shift(forward, "tensor", 1)
        back = shift(back, "tensor", -1)
        for piece, source, at in ((forward, ten - k + n_ten, 0), (back, ten + k, half)):
            base = lax.rem(source, n_ten) * rows + at
            held = [(piece, dp)]
            bit = n_dp // 2
            while bit:
                pairs = [(i, i ^ bit) for i in range(n_dp)]
                held = held + [(lax.ppermute(p, "dp", pairs), who ^ bit) for p, who in held]
                bit //= 2
            for p, who in held:
                full = lax.dynamic_update_slice(full, p, (base + who * part, 0))
    return full


def exchange_columns(array, width, start_of):
    n_seq, me = lax.axis_size("seq"), lax.axis_index("seq")
    rows = array.shape[0]
    result = jnp.zeros((rows * n_seq, width), array.dtype)
    for j in range(n_seq):
        target = lax.rem(me + j, n_seq)
        piece = lax.dynamic_slice(array, (0, start_of(target)), (rows, width))
        if j:
            piece = shift(piece, "seq", j)
        result = lax.dynamic_update_slice(result, piece, (lax.rem(me - j + n_seq, n_seq) * rows, 0))
    return result


def on_device(queries, keys_values, out_weight, residual, segments):
    n_seq, n_ten = lax.axis_size("seq"), lax.axis_size("tensor")
    seq, ten = lax.axis_index("seq"), lax.axis_index("tensor")
    heads_ten = queries.shape[1] // HD
    heads_dev = heads_ten // n_seq
    group_size = H // KVH
    kv_dev = max(1, heads_dev // group_size)
    width = heads_dev * HD

    def kv_start(target):
        return target * heads_dev // group_size * HD

    query = exchange_columns(queries, width, lambda target: target * width)
    keys = exchange_columns(keys_values[:, 0, :], kv_dev * HD, kv_start)
    values_t = exchange_columns(keys_values[:, 1, :], kv_dev * HD, kv_start).T
    rows = query.shape[0]
    positions = jnp.arange(rows, dtype=jnp.int32)
    begins = (positions % L == 0) | (segments != jnp.roll(segments, 1))
    first = lax.cummax(jnp.where(begins, positions, 0))
    first_rows = first.reshape(rows // 512, 512)
    starts = jnp.stack([first_rows[:, 0], first_rows[:, -1]], axis=1).reshape(-1)
    first = jnp.broadcast_to(first[None, :], (8, rows))

    weight = gather_weight(out_weight)

    out_rows = rows // n_ten
    cuts = 2 if heads_dev >= 4 else 1
    count = heads_dev // cuts
    left = jnp.zeros((out_rows, H * HD), jnp.bfloat16)
    for cut in range(cuts):
        blended = attend(starts, query, keys, values_t, first, cut * count, count, group_size)
        for k in range(n_ten):
            target = lax.rem(ten + k, n_ten)
            piece = lax.dynamic_slice(blended, (target * out_rows, 0), (out_rows, count * HD))
            if k:
                piece = shift(piece, "tensor", k)
            base = lax.rem(ten - k + n_ten, n_ten) * heads_ten * HD + cut * count * HD
            for j in range(n_seq):
                held = shift(piece, "seq", j) if j else piece
                source = lax.rem(seq - j + n_seq, n_seq)
                left = lax.dynamic_update_slice(left, held, (0, base + source * width))
    projected = jnp.dot(left, weight, preferred_element_type=jnp.float32)
    return (residual.astype(jnp.float32) + projected).astype(jnp.bfloat16)


def solution(mesh):
    placed = (
        P(("dp", "seq"), "tensor"),
        P(("dp", "seq"), None, "tensor"),
        P("tensor", "seq"),
        P(("dp", "tensor"), "seq"),
        P("dp"),
    )
    return jax.shard_map(
        on_device, mesh=mesh, in_specs=placed, out_specs=P(("dp", "tensor"), "seq"), check_vma=False
    )
```

time: 2000 us -> 688 us (0.34)
  waiting for transfers between devices: 1370 us -> 235 us
  matrix products: 371 us -> 79.7 us
  Pallas kernels: 0 us -> 121 us
  starting transfers between devices: 11.7 us -> 107 us
  other arithmetic: 84.9 us -> 1.16 us
    unnamed x3 -> x0, waiting for transfers between devices: 1100 us -> none
    ppermute x0 -> x41, waiting for transfers between devices: none -> 235 us  [the longest x23 227 us: shift(): lax.ppermute(array, axis, [(i, (i + by) % size) for i in range(size)])]
    all_gather x1 -> x0, waiting for transfers between devices: 200 us -> none  [on_device(): gathered = lax.all_gather(heads_out, 'seq', axis=1, tiled=True)]
    sub x7 -> x0, matrix products: 168 us -> none  [attend(): exponents = jnp.where(allowed, jnp.exp(masked - highest), 0.0)]
    dot_general x10 -> x1, matrix products: 203 us -> 79.7 us  [on_device(): projected = jnp.dot(left, weight, preferred_element_type=jnp.float32)]
    pallas_call x0 -> x2, Pallas kernels: none -> 121 us  [attend(): pl.pallas_call(functools.partial(attend_kernel, block, heads), grid_spec=...]
    ppermute x0 -> x41, starting transfers between devices: none -> 107 us  [the longest x23 83.9 us: shift(): lax.ppermute(array, axis, [(i, (i + by) % size) for i in range(size)])]
    dynamic_update_slice x0 -> x45, local copies, waits for them, and re-layouts: none -> 72.1 us  [the longest x24 40.4 us: gather_weight(): full = lax.dynamic_update_slice(full, p, (base + who * part, 0))]
  transfers between devices with their start and end apart: 4 -> 41, of which waited for: 3 -> 11; matrix products, arithmetic and copies ran while one was open for 7% -> 20% of each run, Pallas kernels for 0% -> 18%
where the time goes in v1:
time: 688 us; the launch traced here: 690 us
  waiting for transfers between devices  235 us (34%)
  local copies, waits for them, and re-layouts  145 us (21%)
  Pallas kernels  121 us (18%)
  starting transfers between devices  107 us (16%)
  matrix products  79.7 us (12%)
    ppermute x23, waiting for transfers between devices, shift(): lax.ppermute(array, axis, [(i, (i + by) % size) for i in range(size)])  227 us
    pallas_call x2, Pallas kernels, attend(): pl.pallas_call(functools.partial(attend_kernel, block, heads), grid_spec=...  121 us
    ppermute x23, starting transfers between devices, shift(): lax.ppermute(array, axis, [(i, (i + by) % size) for i in range(size)])  83.9 us
    dot_general x1, matrix products, on_device(): projected = jnp.dot(left, weight, preferred_element_type=jnp.float32)  79.7 us
    dynamic_update_slice x24, local copies, waits for them, and re-layouts, gather_weight(): full = lax.dynamic_update_slice(full, p, (base + who * part, 0))  40.4 us
    broadcast_in_dim x1, local copies, waits for them, and re-layouts, gather_weight(): full = jnp.zeros((rows * n_ten, columns), out_weight.dtype)  25.9 us
    ppermute x18, starting transfers between devices, gather_weight(): held = held + [(lax.ppermute(p, 'dp', pairs), who ^ bit) for p, who in held]  23.5 us
    dynamic_slice x6, local copies, waits for them, and re-layouts, exchange_columns(): piece = lax.dynamic_slice(array, (0, start_of(target)), (rows, width))  22.3 us
  transfers between devices with their start and end apart: 41, of which 11 were waited for; matrix products, arithmetic and copies ran while one was open for 20% of the time, Pallas kernels for 18%

profile of v1, /device:TPU:19, one launch (start us, length us, event | category | flops | bytes accessed | tf_op | source)
XLA Modules:
  0.0 689.7 jit_solution(7470160669860249755)
XLA Ops:
  0.0 5.0 constant_dynamic-slice_fusion
  10.9 7.8 %constant_dynamic-slice_fusion.14 = (bf16[2048,1024]{1,0:T(8,128)(2,1)}, bf16[4096,1024]{1,0:T(8,128)(2,1)}) fusion(bf16[2048,2048]{1,0:T(8,128)(2,1)} %param.5, s32[]{:T(128)S(6)} %select_n.193, bf16[4096,1024]{1,0:T(8,128)(2,1)} %broadcast_in_dim.18, s32[]{:T(128)S(6)} %select_n.192, s32[]{:T(128)S(6)} %select_n.191), kind=kLoop, calls=%fused_computation.74 | loop fusion | bytes 16777228 | tf_op jit(solution)/shard_map/dynamic_slice | solution.py:137
  23.2 6.7 constant_dynamic-slice_fusion.10
  42.8 25.9 %broadcast_in_dim.20 = bf16[8192,4096]{1,0:T(8,128)(2,1)} broadcast(bf16[]{:T(256)} %constant.104.clone.1), dimensions={} | broadcast | bytes 67108864 | tf_op jit(solution)/shard_map/broadcast_in_dim | solution.py:113
  68.7 6.7 constant_dynamic-update-slice_fusion.24
  75.9 45.2 %collective-permute-done.1 = bf16[2048,128]{0,1:T(8,128)(2,1)} collective-permute-done((bf16[2048,128]{0,1:T(8,128)(2,1)}, bf16[2048,128]{0,1:T(8,128)(2,1)}, u32[]{:S(2)}, u32[]{:S(2)}) %collective-permute-start.1) | collective-permute-done | bytes 524320 | tf_op jit(solution)/shard_map/ppermute | solution.py:102
  122.9 9.5 %collective-permute-done.2 = bf16[2048,128]{0,1:T(8,128)(2,1)} collective-permute-done((bf16[2048,128]{0,1:T(8,128)(2,1)}, bf16[2048,128]{0,1:T(8,128)(2,1)}, u32[]{:S(2)}, u32[]{:S(2)}) %collective-permute-start.2) | collective-permute-done | bytes 524320 | tf_op jit(solution)/shard_map/ppermute | solution.py:102
  146.8 60.5 %shard_map.55 = bf16[4096,512]{1,0:T(8,128)(2,1)S(1)} custom-call(s32[16]{0:T(128)S(1)} %reshape.47.starts_ref, bf16[4096,1024]{1,0:T(8,128)(2,1)} %constant_dynamic-update-slice_fusion.43.q_ref, bf16[4096,128]{1,0:T(8,128)(2,1)S(1)} %copy.27.k_ref, bf16[128,4096]{1,0:T(8,128)(2,1)S(1)} %bitcast.16, s32[8,4096]{1,0:T(8,128)S(1)} %broadcast_in_dim.19.first_ref), custom_call_target="tpu_custom_call" | custom-call | flops 34359738368 | bytes 8388608 | tf_op jit(solution)/shard_map/pallas_call | solution.py:87
  207.3 6.1 broadcast_in_dim.17
  215.9 7.7 %collective-permute-done.22 = bf16[256,4096]{1,0:T(8,128)(2,1)S(1)} collective-permute-done((bf16[256,4096]{1,0:T(8,128)(2,1)}, bf16[256,4096]{1,0:T(8,128)(2,1)S(1)}, u32[]{:S(2)}, u32[]{:S(2)}) %collective-permute-start.22) | collective-permute-done | bytes 2097184 | tf_op jit(solution)/shard_map/ppermute | solution.py:124
  228.3 60.6 %shard_map.56 = bf16[4096,512]{1,0:T(8,128)(2,1)S(1)} custom-call(s32[16]{0:T(128)S(1)} %reshape.47.starts_ref, bf16[4096,1024]{1,0:T(8,128)(2,1)} %constant_dynamic-update-slice_fusion.43.q_ref, bf16[4096,128]{1,0:T(8,128)(2,1)S(1)} %copy.27.k_ref, bf16[128,4096]{1,0:T(8,128)(2,1)S(1)} %bitcast.17, s32[8,4096]{1,0:T(8,128)S(1)} %broadcast_in_dim.19.first_ref), custom_call_target="tpu_custom_call" | custom-call | flops 34359738368 | bytes 8388608 | tf_op jit(solution)/shard_map/pallas_call | solution.py:87
  289.4 5.5 collective-permute-start.24
  304.0 29.8 %collective-permute-done.6 = bf16[1024,512]{1,0:T(8,128)(2,1)S(1)} collective-permute-done((bf16[1024,512]{1,0:T(8,128)(2,1)}, bf16[1024,512]{1,0:T(8,128)(2,1)S(1)}, u32[]{:S(2)}, u32[]{:S(2)}) %collective-permute-start.6) | collective-permute-done | bytes 1048608 | tf_op jit(solution)/shard_map/ppermute | solution.py:102
  338.6 17.8 %collective-permute-done.8 = bf16[1024,512]{1,0:T(8,128)(2,1)S(1)} collective-permute-done((bf16[1024,512]{1,0:T(8,128)(2,1)}, bf16[1024,512]{1,0:T(8,128)(2,1)S(1)}, u32[]{:S(2)}, u32[]{:S(2)}) %collective-permute-start.8) | collective-permute-done | bytes 1048608 | tf_op jit(solution)/shard_map/ppermute | solution.py:102
  363.3 22.2 %collective-permute-start.33 = (bf16[256,4096]{1,0:T(8,128)(2,1)S(1)}, bf16[256,4096]{1,0:T(8,128)(2,1)S(1)}, u32[]{:S(2)}, u32[]{:S(2)}) collective-permute-start(bf16[256,4096]{1,0:T(8,128)(2,1)S(1)} %collective-permute-done.25), channel_id=1, source_target_pairs={{0,1},{1,2},{2,3},{3,0},{4,5},{5,6},{6,7},{7,4},{8,9},{9,10},{10,1... | collective-permute-start | bytes 6291464 | tf_op jit(solution)/shard_map/ppermute | solution.py:102
  389.3 11.1 %collective-permute-done.9 = bf16[1024,512]{1,0:T(8,128)(2,1)S(1)} collective-permute-done((bf16[1024,512]{1,0:T(8,128)(2,1)S(1)}, bf16[1024,512]{1,0:T(8,128)(2,1)S(1)}, u32[]{:S(2)}, u32[]{:S(2)}) %collective-permute-start.9) | collective-permute-done | bytes 1048608 | tf_op jit(solution)/shard_map/ppermute | solution.py:102
  400.4 28.3 %collective-permute-start.37 = (bf16[256,4096]{1,0:T(8,128)(2,1)S(1)}, bf16[256,4096]{1,0:T(8,128)(2,1)S(1)}, u32[]{:S(2)}, u32[]{:S(2)}) collective-permute-start(bf16[256,4096]{1,0:T(8,128)(2,1)S(1)} %collective-permute-done.29), channel_id=1, source_target_pairs={{0,3},{1,0},{2,1},{3,2},{4,7},{5,4},{6,5},{7,6},{8,11},{9,8},{10,9... | collective-permute-start | bytes 6291464 | tf_op jit(solution)/shard_map/ppermute | solution.py:102
  438.6 18.7 %collective-permute-start.11 = (bf16[1024,512]{1,0:T(8,128)(2,1)S(1)}, bf16[1024,512]{1,0:T(8,128)(2,1)S(1)}, u32[]{:S(2)}, u32[]{:S(2)}) collective-permute-start(bf16[1024,512]{1,0:T(8,128)(2,1)S(1)} %get-tuple-element.15), channel_id=1, source_target_pairs={{0,1},{1,2},{2,3},{3,0},{4,5},{5,6},{6,7},{7,4},{8,9},{9,10},{10,1... | collective-permute-start | bytes 3145736 | tf_op jit(solution)/shard_map/ppermute | solution.py:102
  458.9 17.3 %collective-permute-done.37 = bf16[256,4096]{1,0:T(8,128)(2,1)S(1)} collective-permute-done((bf16[256,4096]{1,0:T(8,128)(2,1)S(1)}, bf16[256,4096]{1,0:T(8,128)(2,1)S(1)}, u32[]{:S(2)}, u32[]{:S(2)}) %collective-permute-start.37) | collective-permute-done | bytes 2097184 | tf_op jit(solution)/shard_map/ppermute | solution.py:102
  481.3 19.9 %collective-permute-done.11 = bf16[1024,512]{1,0:T(8,128)(2,1)S(1)} collective-permute-done((bf16[1024,512]{1,0:T(8,128)(2,1)S(1)}, bf16[1024,512]{1,0:T(8,128)(2,1)S(1)}, u32[]{:S(2)}, u32[]{:S(2)}) %collective-permute-start.11) | collective-permute-done | bytes 1048608 | tf_op jit(solution)/shard_map/ppermute | solution.py:102
  507.3 39.6 %collective-permute-done.13 = bf16[1024,512]{1,0:T(8,128)(2,1)S(1)} collective-permute-done((bf16[1024,512]{1,0:T(8,128)(2,1)S(1)}, bf16[1024,512]{1,0:T(8,128)(2,1)S(1)}, u32[]{:S(2)}, u32[]{:S(2)}) %collective-permute-start.13) | collective-permute-done | bytes 1048608 | tf_op jit(solution)/shard_map/ppermute | solution.py:102
  556.7 19.3 %collective-permute-done.15 = bf16[1024,512]{1,0:T(8,128)(2,1)S(1)} collective-permute-done((bf16[1024,512]{1,0:T(8,128)(2,1)S(1)}, bf16[1024,512]{1,0:T(8,128)(2,1)S(1)}, u32[]{:S(2)}, u32[]{:S(2)}) %collective-permute-start.15) | collective-permute-done | bytes 1048608 | tf_op jit(solution)/shard_map/ppermute | solution.py:102
  583.8 17.5 %collective-permute-done.16 = bf16[1024,512]{1,0:T(8,128)(2,1)S(1)} collective-permute-done((bf16[1024,512]{1,0:T(8,128)(2,1)S(1)}, bf16[1024,512]{1,0:T(8,128)(2,1)S(1)}, u32[]{:S(2)}, u32[]{:S(2)}) %collective-permute-start.16) | collective-permute-done | bytes 1048608 | tf_op jit(solution)/shard_map/ppermute | solution.py:102
  610.0 79.7 %add_convert_fusion = bf16[1024,4096]{1,0:T(8,128)(2,1)} fusion(bf16[1024,4096]{1,0:T(8,128)(2,1)S(1)} %bitcast.24, bf16[1024,8192]{1,0:T(8,128)(2,1)} %constant_dynamic-update-slice_fusion.25, bf16[8192,4096]{1,0:T(8,128)(2,1)} %constant_dynamic-update-slice_fusion), kind=kOutput, calls=%fused_computation | convolution fusion | flops 68732059648 | bytes 100663296 | tf_op jit(solution)/shard_map/dot_general | solution.py:185
  (156 shorter events, 120.9 us)
Async XLA Ops:
  5.0 128.5 %collective-permute-start.17 = (bf16[256,4096]{1,0:T(8,128)(2,1)}, bf16[256,4096]{1,0:T(8,128)(2,1)}, u32[]{:S(2)}, u32[]{:S(2)}) collective-permute-start(bf16[256,4096]{1,0:T(8,128)(2,1)} %get-tuple-element.10), channel_id=1, source_target_pairs={{0,1},{1,2},{2,3},{3,0},{4,5},{5,6},{6,7},{7,4},{8,9},{9,10},{10,1... | collective-permute-start | bytes 6291464 | tf_op jit(solution)/shard_map/ppermute | solution.py:102
  6.3 130.9 %collective-permute-start.21 = (bf16[256,4096]{1,0:T(8,128)(2,1)}, bf16[256,4096]{1,0:T(8,128)(2,1)}, u32[]{:S(2)}, u32[]{:S(2)}) collective-permute-start(bf16[256,4096]{1,0:T(8,128)(2,1)} %get-tuple-element.9), channel_id=1, source_target_pairs={{0,3},{1,0},{2,1},{3,2},{4,7},{5,4},{6,5},{7,6},{8,11},{9,8},{10,9... | collective-permute-start | bytes 6291464 | tf_op jit(solution)/shard_map/ppermute | solution.py:102
  18.8 122.1 %collective-permute-start = (bf16[2048,1024]{1,0:T(8,128)(2,1)}, bf16[2048,1024]{1,0:T(8,128)(2,1)}, u32[]{:S(2)}, u32[]{:S(2)}) collective-permute-start(bf16[2048,1024]{1,0:T(8,128)(2,1)} %get-tuple-element.11), channel_id=1, source_target_pairs={{0,4},{4,0},{1,5},{5,1},{2,6},{6,2},{3,7},{7,3},{8,12},{12,8},{9,1... | collective-permute-start | bytes 12582920 | tf_op jit(solution)/shard_map/ppermute | solution.py:102
  33.4 87.8 %collective-permute-start.1 = (bf16[2048,128]{0,1:T(8,128)(2,1)}, bf16[2048,128]{0,1:T(8,128)(2,1)}, u32[]{:S(2)}, u32[]{:S(2)}) collective-permute-start(bf16[2048,128]{0,1:T(8,128)(2,1)} %bitcast.21), channel_id=1, source_target_pairs={{0,4},{4,0},{1,5},{5,1},{2,6},{6,2},{3,7},{7,3},{8,12},{12,8},{9,1... | collective-permute-start | bytes 1572872 | tf_op jit(solution)/shard_map/ppermute | solution.py:102
  36.4 95.9 %collective-permute-start.2 = (bf16[2048,128]{0,1:T(8,128)(2,1)}, bf16[2048,128]{0,1:T(8,128)(2,1)}, u32[]{:S(2)}, u32[]{:S(2)}) collective-permute-start(bf16[2048,128]{0,1:T(8,128)(2,1)} %bitcast.20), channel_id=1, source_target_pairs={{0,4},{4,0},{1,5},{5,1},{2,6},{6,2},{3,7},{7,3},{8,12},{12,8},{9,1... | collective-permute-start | bytes 1572872 | tf_op jit(solution)/shard_map/ppermute | solution.py:102
  133.5 82.0 %collective-permute-start.18 = (bf16[256,4096]{1,0:T(8,128)(2,1)}, bf16[256,4096]{1,0:T(8,128)(2,1)S(1)}, u32[]{:S(2)}, u32[]{:S(2)}) collective-permute-start(bf16[256,4096]{1,0:T(8,128)(2,1)} %collective-permute-done.17), channel_id=1, source_target_pairs={{0,16},{8,24},{16,0},{24,8},{1,17},{9,25},{17,1},{25,9},{2,18},{10... | collective-permute-start | bytes 6291464 | tf_op jit(solution)/shard_map/ppermute | solution.py:124
  134.8 80.9 %collective-permute-start.19 = (bf16[256,4096]{1,0:T(8,128)(2,1)}, bf16[256,4096]{1,0:T(8,128)(2,1)S(1)}, u32[]{:S(2)}, u32[]{:S(2)}) collective-permute-start(bf16[256,4096]{1,0:T(8,128)(2,1)} %collective-permute-done.17), channel_id=1, source_target_pairs={{0,8},{8,0},{16,24},{24,16},{1,9},{9,1},{17,25},{25,17},{2,10},{10... | collective-permute-start | bytes 6291464 | tf_op jit(solution)/shard_map/ppermute | solution.py:124
  137.2 86.4 %collective-permute-start.22 = (bf16[256,4096]{1,0:T(8,128)(2,1)}, bf16[256,4096]{1,0:T(8,128)(2,1)S(1)}, u32[]{:S(2)}, u32[]{:S(2)}) collective-permute-start(bf16[256,4096]{1,0:T(8,128)(2,1)} %collective-permute-done.21), channel_id=1, source_target_pairs={{0,16},{8,24},{16,0},{24,8},{1,17},{9,25},{17,1},{25,9},{2,18},{10... | collective-permute-start | bytes 6291464 | tf_op jit(solution)/shard_map/ppermute | solution.py:124
  137.4 87.5 %collective-permute-start.23 = (bf16[256,4096]{1,0:T(8,128)(2,1)}, bf16[256,4096]{1,0:T(8,128)(2,1)S(1)}, u32[]{:S(2)}, u32[]{:S(2)}) collective-permute-start(bf16[256,4096]{1,0:T(8,128)(2,1)} %collective-permute-done.21), channel_id=1, source_target_pairs={{0,8},{8,0},{16,24},{24,16},{1,9},{9,1},{17,25},{25,17},{2,10},{10... | collective-permute-start | bytes 6291464 | tf_op jit(solution)/shard_map/ppermute | solution.py:124
  140.9 148.0 %collective-permute-start.25 = (bf16[256,4096]{1,0:T(8,128)(2,1)}, bf16[256,4096]{1,0:T(8,128)(2,1)S(1)}, u32[]{:S(2)}, u32[]{:S(2)}) collective-permute-start(bf16[256,4096]{1,0:T(8,128)(2,1)} %collective-permute-done.17), channel_id=1, source_target_pairs={{0,1},{1,2},{2,3},{3,0},{4,5},{5,6},{6,7},{7,4},{8,9},{9,10},{10,1... | collective-permute-start | bytes 6291464 | tf_op jit(solution)/shard_map/ppermute | solution.py:102
  215.5 121.4 %collective-permute-start.29 = (bf16[256,4096]{1,0:T(8,128)(2,1)}, bf16[256,4096]{1,0:T(8,128)(2,1)S(1)}, u32[]{:S(2)}, u32[]{:S(2)}) collective-permute-start(bf16[256,4096]{1,0:T(8,128)(2,1)} %collective-permute-done.21), channel_id=1, source_target_pairs={{0,3},{1,0},{2,1},{3,2},{4,7},{5,4},{6,5},{7,6},{8,11},{9,8},{10,9... | collective-permute-start | bytes 6291464 | tf_op jit(solution)/shard_map/ppermute | solution.py:102
  215.7 73.7 %collective-permute-start.3 = (bf16[1024,512]{1,0:T(8,128)(2,1)S(1)}, bf16[1024,512]{1,0:T(8,128)(2,1)}, u32[]{:S(2)}, u32[]{:S(2)}) collective-permute-start(bf16[1024,512]{1,0:T(8,128)(2,1)S(1)} %get-tuple-element.22), channel_id=1, source_target_pairs={{0,4},{4,0},{1,5},{5,1},{2,6},{6,2},{3,7},{7,3},{8,12},{12,8},{9,1... | collective-permute-start | bytes 3145736 | tf_op jit(solution)/shard_map/ppermute | solution.py:102
  223.6 72.8 %collective-permute-start.4 = (bf16[1024,512]{1,0:T(8,128)(2,1)}, bf16[1024,512]{1,0:T(8,128)(2,1)S(1)}, u32[]{:S(2)}, u32[]{:S(2)}) collective-permute-start(bf16[1024,512]{1,0:T(8,128)(2,1)} %get-tuple-element.20), channel_id=1, source_target_pairs={{0,1},{1,2},{2,3},{3,0},{4,5},{5,6},{6,7},{7,4},{8,9},{9,10},{10,1... | collective-permute-start | bytes 3145736 | tf_op jit(solution)/shard_map/ppermute | solution.py:102
  224.9 109.4 %collective-permute-start.20 = (bf16[256,4096]{1,0:T(8,128)(2,1)S(1)}, bf16[256,4096]{1,0:T(8,128)(2,1)S(1)}, u32[]{:S(2)}, u32[]{:S(2)}) collective-permute-start(bf16[256,4096]{1,0:T(8,128)(2,1)S(1)} %collective-permute-done.18), channel_id=1, source_target_pairs={{0,8},{8,0},{16,24},{24,16},{1,9},{9,1},{17,25},{25,17},{2,10},{10... | collective-permute-start | bytes 6291464 | tf_op jit(solution)/shard_map/ppermute | solution.py:124
  289.4 71.9 %collective-permute-start.24 = (bf16[256,4096]{1,0:T(8,128)(2,1)S(1)}, bf16[256,4096]{1,0:T(8,128)(2,1)S(1)}, u32[]{:S(2)}, u32[]{:S(2)}) collective-permute-start(bf16[256,4096]{1,0:T(8,128)(2,1)S(1)} %collective-permute-done.22), channel_id=1, source_target_pairs={{0,8},{8,0},{16,24},{24,16},{1,9},{9,1},{17,25},{25,17},{2,10},{10... | collective-permute-start | bytes 6291464 | tf_op jit(solution)/shard_map/ppermute | solution.py:124
  336.9 96.4 %collective-permute-start.26 = (bf16[256,4096]{1,0:T(8,128)(2,1)S(1)}, bf16[256,4096]{1,0:T(8,128)(2,1)S(1)}, u32[]{:S(2)}, u32[]{:S(2)}) collective-permute-start(bf16[256,4096]{1,0:T(8,128)(2,1)S(1)} %collective-permute-done.25), channel_id=1, source_target_pairs={{0,16},{8,24},{16,0},{24,8},{1,17},{9,25},{17,1},{25,9},{2,18},{10... | collective-permute-start | bytes 6291464 | tf_op jit(solution)/shard_map/ppermute | solution.py:124
  356.3 78.6 %collective-permute-start.27 = (bf16[256,4096]{1,0:T(8,128)(2,1)S(1)}, bf16[256,4096]{1,0:T(8,128)(2,1)S(1)}, u32[]{:S(2)}, u32[]{:S(2)}) collective-permute-start(bf16[256,4096]{1,0:T(8,128)(2,1)S(1)} %collective-permute-done.25), channel_id=1, source_target_pairs={{0,8},{8,0},{16,24},{24,16},{1,9},{9,1},{17,25},{25,17},{2,10},{10... | collective-permute-start | bytes 6291464 | tf_op jit(solution)/shard_map/ppermute | solution.py:124
  363.3 75.3 %collective-permute-start.33 = (bf16[256,4096]{1,0:T(8,128)(2,1)S(1)}, bf16[256,4096]{1,0:T(8,128)(2,1)S(1)}, u32[]{:S(2)}, u32[]{:S(2)}) collective-permute-start(bf16[256,4096]{1,0:T(8,128)(2,1)S(1)} %collective-permute-done.25), channel_id=1, source_target_pairs={{0,1},{1,2},{2,3},{3,0},{4,5},{5,6},{6,7},{7,4},{8,9},{9,10},{10,1... | collective-permute-start | bytes 6291464 | tf_op jit(solution)/shard_map/ppermute | solution.py:102
  400.4 75.8 %collective-permute-start.37 = (bf16[256,4096]{1,0:T(8,128)(2,1)S(1)}, bf16[256,4096]{1,0:T(8,128)(2,1)S(1)}, u32[]{:S(2)}, u32[]{:S(2)}) collective-permute-start(bf16[256,4096]{1,0:T(8,128)(2,1)S(1)} %collective-permute-done.29), channel_id=1, source_target_pairs={{0,3},{1,0},{2,1},{3,2},{4,7},{5,4},{6,5},{7,6},{8,11},{9,8},{10,9... | collective-permute-start | bytes 6291464 | tf_op jit(solution)/shard_map/ppermute | solution.py:102
  433.3 69.0 %collective-permute-start.28 = (bf16[256,4096]{1,0:T(8,128)(2,1)S(1)}, bf16[256,4096]{1,0:T(8,128)(2,1)S(1)}, u32[]{:S(2)}, u32[]{:S(2)}) collective-permute-start(bf16[256,4096]{1,0:T(8,128)(2,1)S(1)} %collective-permute-done.26), channel_id=1, source_target_pairs={{0,8},{8,0},{16,24},{24,16},{1,9},{9,1},{17,25},{25,17},{2,10},{10... | collective-permute-start | bytes 6291464 | tf_op jit(solution)/shard_map/ppermute | solution.py:124
  438.3 67.1 %collective-permute-start.31 = (bf16[256,4096]{1,0:T(8,128)(2,1)S(1)}, bf16[256,4096]{1,0:T(8,128)(2,1)S(1)}, u32[]{:S(2)}, u32[]{:S(2)}) collective-permute-start(bf16[256,4096]{1,0:T(8,128)(2,1)S(1)} %collective-permute-done.29), channel_id=1, source_target_pairs={{0,8},{8,0},{16,24},{24,16},{1,9},{9,1},{17,25},{25,17},{2,10},{10... | collective-permute-start | bytes 6291464 | tf_op jit(solution)/shard_map/ppermute | solution.py:124
  476.2 72.0 %collective-permute-start.32 = (bf16[256,4096]{1,0:T(8,128)(2,1)S(1)}, bf16[256,4096]{1,0:T(8,128)(2,1)S(1)}, u32[]{:S(2)}, u32[]{:S(2)}) collective-permute-start(bf16[256,4096]{1,0:T(8,128)(2,1)S(1)} %collective-permute-done.30), channel_id=1, source_target_pairs={{0,8},{8,0},{16,24},{24,16},{1,9},{9,1},{17,25},{25,17},{2,10},{10... | collective-permute-start | bytes 6291464 | tf_op jit(solution)/shard_map/ppermute | solution.py:124
  478.6 71.9 %collective-permute-start.34 = (bf16[256,4096]{1,0:T(8,128)(2,1)S(1)}, bf16[256,4096]{1,0:T(8,128)(2,1)S(1)}, u32[]{:S(2)}, u32[]{:S(2)}) collective-permute-start(bf16[256,4096]{1,0:T(8,128)(2,1)S(1)} %collective-permute-done.33), channel_id=1, source_target_pairs={{0,16},{8,24},{16,0},{24,8},{1,17},{9,25},{17,1},{25,9},{2,18},{10... | collective-permute-start | bytes 6291464 | tf_op jit(solution)/shard_map/ppermute | solution.py:124
  501.2 75.3 %collective-permute-start.38 = (bf16[256,4096]{1,0:T(8,128)(2,1)S(1)}, bf16[256,4096]{1,0:T(8,128)(2,1)S(1)}, u32[]{:S(2)}, u32[]{:S(2)}) collective-permute-start(bf16[256,4096]{1,0:T(8,128)(2,1)S(1)} %collective-permute-done.37), channel_id=1, source_target_pairs={{0,16},{8,24},{16,0},{24,8},{1,17},{9,25},{17,1},{25,9},{2,18},{10... | collective-permute-start | bytes 6291464 | tf_op jit(solution)/shard_map/ppermute | solution.py:124
  (25 other events, 888.9 us)

commit v2 on v1

--- a/solution.py
+++ b/solution.py
@@ -72,7 +72,7 @@
         num_scalar_prefetch=1,
         grid=(count // heads, blocks),
         in_specs=[
-            pl.BlockSpec((block, heads * HD), lambda h, b, s: (b, head0 // heads + h)),
+            pl.BlockSpec((block, heads * HD), lambda h, b, s: (b, h)),
             pl.BlockSpec((rows, HD), lambda h, b, s: (0, (head0 + h * heads) // group_size)),
             pl.BlockSpec((HD, rows), lambda h, b, s: ((head0 + h * heads) // group_size, 0)),
             pl.BlockSpec((8, block), lambda h, b, s: (0, b)),
@@ -102,29 +102,33 @@
     return lax.ppermute(array, axis, [(i, (i + by) % size) for i in range(size)])
 
 
-def gather_weight(out_weight):
+def share_of(mine):
+    part = mine.shape[0] // lax.axis_size("dp")
+    return lax.dynamic_slice(mine, (lax.axis_index("dp") * part, 0), (part, mine.shape[1]))
+
+
+def spread_weight(mine, gathered):
     n_dp, n_ten = lax.axis_size("dp"), lax.axis_size("tensor")
     dp, ten = lax.axis_index("dp"), lax.axis_index("tensor")
-    rows, columns = out_weight.shape
+    rows, columns = mine.shape
     part = rows // n_dp
-    half = part // 2
-    forward = lax.dynamic_slice(out_weight, (dp * part, 0), (half, columns))
-    back = lax.dynamic_slice(out_weight, (dp * part + half, 0), (half, columns))
-    full = jnp.zeros((rows * n_ten, columns), out_weight.dtype)
-    full = lax.dynamic_update_slice(full, out_weight, (ten * rows, 0))
-    for k in range(1, n_ten):
-        forward = shift(forward, "tensor", 1)
-        back = shift(back, "tensor", -1)
-        for piece, source, at in ((forward, ten - k + n_ten, 0), (back, ten + k, half)):
-            base = lax.rem(source, n_ten) * rows + at
-            held = [(piece, dp)]
-            bit = n_dp // 2
-            while bit:
-                pairs = [(i, i ^ bit) for i in range(n_dp)]
-                held = held + [(lax.ppermute(p, "dp", pairs), who ^ bit) for p, who in held]
-                bit //= 2
-            for p, who in held:
-                full = lax.dynamic_update_slice(full, p, (base + who * part, 0))
+    others = [lax.rem(ten + k, n_ten) for k in range(1, n_ten)]
+    piece = jnp.concatenate(
+        [lax.dynamic_slice(gathered, (other * part, 0), (part, columns)) for other in others]
+    )
+    held = [(piece, dp)]
+    bit = n_dp // 2
+    while bit:
+        pairs = [(i, i ^ bit) for i in range(n_dp)]
+        held = held + [(lax.ppermute(p, "dp", pairs), who ^ bit) for p, who in held]
+        bit //= 2
+    full = jnp.zeros((rows * n_ten, columns), mine.dtype)
+    full = lax.dynamic_update_slice(full, mine, (ten * rows, 0))
+    for p, who in held:
+        for at, other in enumerate(others):
+            full = lax.dynamic_update_slice(
+                full, p[at * part : (at + 1) * part], (other * rows + who * part, 0)
+            )
     return full
 
 
@@ -153,10 +157,9 @@
     def kv_start(target):
         return target * heads_dev // group_size * HD
 
-    query = exchange_columns(queries, width, lambda target: target * width)
     keys = exchange_columns(keys_values[:, 0, :], kv_dev * HD, kv_start)
     values_t = exchange_columns(keys_values[:, 1, :], kv_dev * HD, kv_start).T
-    rows = query.shape[0]
+    rows = keys.shape[0]
     positions = jnp.arange(rows, dtype=jnp.int32)
     begins = (positions % L == 0) | (segments != jnp.roll(segments, 1))
     first = lax.cummax(jnp.where(begins, positions, 0))
@@ -164,26 +167,39 @@
     starts = jnp.stack([first_rows[:, 0], first_rows[:, -1]], axis=1).reshape(-1)
     first = jnp.broadcast_to(first[None, :], (8, rows))
 
-    weight = gather_weight(out_weight)
-
     out_rows = rows // n_ten
     cuts = 2 if heads_dev >= 4 else 1
     count = heads_dev // cuts
-    left = jnp.zeros((out_rows, H * HD), jnp.bfloat16)
+    cut_width = count * HD
+    by_cut = out_weight.reshape(n_seq, cuts, cut_width, out_weight.shape[1])
+    mine = [by_cut[:, cut].reshape(n_seq * cut_width, out_weight.shape[1]) for cut in range(cuts)]
+    gathered = lax.all_gather(share_of(mine[0]), "tensor", axis=0, tiled=True)
+    total = residual.astype(jnp.float32)
     for cut in range(cuts):
+        held_queries = lax.optimization_barrier((queries, keys))[0] if cut else queries
+        query = exchange_columns(
+            held_queries, cut_width, lambda target: target * width + cut * cut_width
+        )
         blended = attend(starts, query, keys, values_t, first, cut * count, count, group_size)
+        gathered = lax.optimization_barrier((gathered, blended))[0]
+        ready = gathered
+        if cut + 1 < cuts:
+            share = lax.optimization_barrier((share_of(mine[cut + 1]), gathered))[0]
+            gathered = lax.all_gather(share, "tensor", axis=0, tiled=True)
+        weight = spread_weight(mine[cut], ready)
+        left = jnp.zeros((out_rows, n_ten * n_seq * cut_width), jnp.bfloat16)
         for k in range(n_ten):
             target = lax.rem(ten + k, n_ten)
-            piece = lax.dynamic_slice(blended, (target * out_rows, 0), (out_rows, count * HD))
+            piece = lax.dynamic_slice(blended, (target * out_rows, 0), (out_rows, cut_width))
             if k:
                 piece = shift(piece, "tensor", k)
-            base = lax.rem(ten - k + n_ten, n_ten) * heads_ten * HD + cut * count * HD
+            base = lax.rem(ten - k + n_ten, n_ten) * n_seq * cut_width
             for j in range(n_seq):
                 held = shift(piece, "seq", j) if j else piece
                 source = lax.rem(seq - j + n_seq, n_seq)
-                left = lax.dynamic_update_slice(left, held, (0, base + source * width))
-    projected = jnp.dot(left, weight, preferred_element_type=jnp.float32)
-    return (residual.astype(jnp.float32) + projected).astype(jnp.bfloat16)
+                left = lax.dynamic_update_slice(left, held, (0, base + source * cut_width))
+        total = total + jnp.dot(left, weight, preferred_element_type=jnp.float32)
+    return total.astype(jnp.bfloat16)
 
 
 def solution(mesh):

time: 688 us -> 881 us (1.28); the launches traced: 690 us -> 871 us
  waiting for transfers between devices: 235 us -> 402 us
  starting transfers between devices: 107 us -> 24.2 us
  local copies, waits for them, and re-layouts: 145 us -> 211 us
  between operations: 0.49 us -> 14.2 us
  other arithmetic: 1.16 us -> 12 us
    ppermute x18 -> x6, waiting for transfers between devices: 7.74 us -> 113 us  [spread_weight(): held = held + [(lax.ppermute(p, 'dp', pairs), who ^ bit) for p, who in held]]
    ppermute x23 -> x18, starting transfers between devices: 83.9 us -> 17 us  [shift(): lax.ppermute(array, axis, [(i, (i + by) % size) for i in range(size)])]
    ppermute x23 -> x18, waiting for transfers between devices: 227 us -> 282 us  [shift(): lax.ppermute(array, axis, [(i, (i + by) % size) for i in range(size)])]
    dynamic_update_slice x39 -> x40, local copies, waits for them, and re-layouts: 63.5 us -> 115 us  [the longest x24 73.9 us: spread_weight(): lax.dynamic_update_slice(full, p[at * part:(at + 1) * part], (other * row...]
    broadcast_in_dim x3 -> x0, local copies, waits for them, and re-layouts: 36.4 us -> none  [the longest x1 25.9 us: gather_weight(): full = jnp.zeros((rows * n_ten, columns), out_weight.dtype)]
    another operation x8 -> x14, local copies, waits for them, and re-layouts: 0.68 us -> 33.5 us
    ppermute x18 -> x6, starting transfers between devices: 23.5 us -> 7.14 us  [spread_weight(): held = held + [(lax.ppermute(p, 'dp', pairs), who ^ bit) for p, who in held]]
    slice x0 -> x1, local copies, waits for them, and re-layouts: none -> 11.8 us  [on_device(): by_cut[:, cut].reshape(n_seq * cut_width, out_weight.shape[1])]
  transfers between devices with their start and end apart: 41 -> 26, of which waited for: 11 -> 11; matrix products, arithmetic and copies ran while one was open for 20% -> 27% of each run, Pallas kernels for 18% -> 14%
where the time goes in v2:
time: 881 us; the launch traced here: 871 us
  waiting for transfers between devices  402 us (46%)
  local copies, waits for them, and re-layouts  211 us (24%)
  Pallas kernels  121 us (14%)
  matrix products  86.6 us (10%)
  starting transfers between devices  24.2 us (3%)
  between operations  14.2 us (2%)
  other arithmetic  12 us (1%)
    ppermute x18, waiting for transfers between devices, shift(): lax.ppermute(array, axis, [(i, (i + by) % size) for i in range(size)])  282 us
    pallas_call x2, Pallas kernels, attend(): pl.pallas_call(functools.partial(attend_kernel, block, heads), grid_spec=...  121 us
    ppermute x6, waiting for transfers between devices, spread_weight(): held = held + [(lax.ppermute(p, 'dp', pairs), who ^ bit) for p, who in held]  113 us
    dot_general x2, matrix products, on_device(): total = total + jnp.dot(left, weight, preferred_element_type=jnp.float32)  86.6 us
    dynamic_update_slice x24, local copies, waits for them, and re-layouts, spread_weight(): lax.dynamic_update_slice(full, p[at * part:(at + 1) * part], (other * row...  73.9 us
    another operation x14, local copies, waits for them, and re-layouts  33.5 us
    dynamic_update_slice x14, local copies, waits for them, and re-layouts, on_device(): left = lax.dynamic_update_slice(left, held, (0, base + source * cut_width))  25 us
    dynamic_slice x7, local copies, waits for them, and re-layouts, exchange_columns(): piece = lax.dynamic_slice(array, (0, start_of(target)), (rows, width))  22.2 us
  transfers between devices with their start and end apart: 26, of which 11 were waited for; matrix products, arithmetic and copies ran while one was open for 27% of the time, Pallas kernels for 14%

profile of v2, /device:TPU:19, one launch (start us, length us, event | category | flops | bytes accessed | tf_op | source)
XLA Modules:
  0.0 871.0 jit_solution(2387106899386512303)
XLA Ops:
  6.5 11.8 %fusion.5 = (bf16[2,1,512,4096]{3,2,1,0:T(8,128)(2,1)}, bf16[2,1,512,4096]{3,2,1,0:T(8,128)(2,1)}) fusion(bf16[2,2,512,4096]{3,2,1,0:T(8,128)(2,1)} %bitcast.27), kind=kLoop, calls=%fused_computation.88 | loop fusion | bytes 33554432 | tf_op jit(solution)/shard_map/slice | solution.py:175
  23.9 4.6 constant_dynamic-slice_fusion.21
  31.7 5.2 constant_dynamic-slice_fusion.17
  53.2 33.3 %collective-permute-done.1 = bf16[2048,128]{0,1:T(8,128)(2,1)} collective-permute-done((bf16[2048,128]{0,1:T(8,128)(2,1)}, bf16[2048,128]{0,1:T(8,128)(2,1)}, u32[]{:S(2)}, u32[]{:S(2)}) %collective-permute-start.1) | collective-permute-done | bytes 524320 | tf_op jit(solution)/shard_map/ppermute | solution.py:102
  90.7 4.6 constant_dynamic-slice_fusion.8
  101.9 60.5 %shard_map.55 = bf16[4096,512]{1,0:T(8,128)(2,1)S(1)} custom-call(s32[16]{0:T(128)S(1)} %reshape.50.starts_ref, bf16[4096,512]{1,0:T(8,128)(2,1)} %constant_dynamic-update-slice_fusion.27.q_ref, bf16[4096,128]{1,0:T(8,128)(2,1)S(1)} %copy.27.k_ref, bf16[128,4096]{1,0:T(8,128)(2,1)S(1)} %bitcast.21, s32[8,4096]{1,0:T(8,128)S(1)} %broadcast_in_dim.4.first_ref), custom_call_target="tpu_custom_call" | custom-call | flops 34359738368 | bytes 8388608 | tf_op jit(solution)/shard_map/pallas_call | solution.py:87
  164.3 6.2 all-gather.3.cloned.1.call-done
  170.6 11.8 %broadcast.44.clone = bf16[4096,4096]{1,0:T(8,128)(2,1)} broadcast(bf16[]{:T(256)} %constant.103.clone.1), dimensions={} | broadcast | bytes 33554432 | tf_op jit(solution)/shard_map/broadcast.7
  182.4 8.5 constant_dynamic-update-slice_fusion.16
  210.4 9.5 %pad_maximum_fusion = bf16[768,4096]{1,0:T(8,128)(2,1)} fusion(bf16[256,4096]{1,0:T(8,128)(2,1)S(1)} %get-tuple-element.14, bf16[256,4096]{1,0:T(8,128)(2,1)S(1)} %get-tuple-element.16, bf16[256,4096]{1,0:T(8,128)(2,1)S(1)} %get-tuple-element.18), kind=kLoop, calls=%fused_computation.1 | loop fusion | flops 18874368 | bytes 12582912 | tf_op jit(solution)/shard_map/concatenate | solution.py:116
  220.9 60.5 %shard_map.56 = bf16[4096,512]{1,0:T(8,128)(2,1)S(1)} custom-call(s32[16]{0:T(128)S(1)} %reshape.50.starts_ref, bf16[4096,512]{1,0:T(8,128)(2,1)} %constant_dynamic-update-slice_fusion.12.q_ref, bf16[4096,128]{1,0:T(8,128)(2,1)S(1)} %copy.27.k_ref, bf16[128,4096]{1,0:T(8,128)(2,1)S(1)} %bitcast.22, s32[8,4096]{1,0:T(8,128)S(1)} %broadcast_in_dim.4.first_ref), custom_call_target="tpu_custom_call" | custom-call | flops 34359738368 | bytes 8388608 | tf_op jit(solution)/shard_map/pallas_call | solution.py:87
  281.4 4.3 broadcast.39.clone.1
  288.7 29.9 %collective-permute-done.6 = bf16[1024,512]{1,0:T(8,128)(2,1)} collective-permute-done((bf16[1024,512]{1,0:T(8,128)(2,1)}, bf16[1024,512]{1,0:T(8,128)(2,1)}, u32[]{:S(2)}, u32[]{:S(2)}) %collective-permute-start.6) | collective-permute-done | bytes 1048608 | tf_op jit(solution)/shard_map/ppermute | solution.py:102
  321.7 114.9 %collective-permute-done.8 = bf16[1024,512]{1,0:T(8,128)(2,1)S(1)} collective-permute-done((bf16[1024,512]{1,0:T(8,128)(2,1)}, bf16[1024,512]{1,0:T(8,128)(2,1)S(1)}, u32[]{:S(2)}, u32[]{:S(2)}) %collective-permute-start.8) | collective-permute-done | bytes 1048608 | tf_op jit(solution)/shard_map/ppermute | solution.py:102
  439.1 36.6 %collective-permute-done.15 = bf16[1024,512]{1,0:T(8,128)(2,1)S(1)} collective-permute-done((bf16[1024,512]{1,0:T(8,128)(2,1)S(1)}, bf16[1024,512]{1,0:T(8,128)(2,1)S(1)}, u32[]{:S(2)}, u32[]{:S(2)}) %collective-permute-start.15) | collective-permute-done | bytes 1048608 | tf_op jit(solution)/shard_map/ppermute | solution.py:102
  477.3 11.1 %broadcast.44.clone.1 = bf16[4096,4096]{1,0:T(8,128)(2,1)} broadcast(bf16[]{:T(256)} %constant.103.clone.1), dimensions={} | broadcast | bytes 33554432 | tf_op jit(solution)/shard_map/broadcast.7
  488.3 7.7 constant_dynamic-update-slice_fusion.3
  512.3 10.4 %collective-permute-done.9 = bf16[1024,512]{1,0:T(8,128)(2,1)} collective-permute-done((bf16[1024,512]{1,0:T(8,128)(2,1)S(1)}, bf16[1024,512]{1,0:T(8,128)(2,1)}, u32[]{:S(2)}, u32[]{:S(2)}) %collective-permute-start.9) | collective-permute-done | bytes 1048608 | tf_op jit(solution)/shard_map/ppermute | solution.py:102
  530.6 14.5 %collective-permute-done.16 = bf16[1024,512]{1,0:T(8,128)(2,1)S(1)} collective-permute-done((bf16[1024,512]{1,0:T(8,128)(2,1)}, bf16[1024,512]{1,0:T(8,128)(2,1)S(1)}, u32[]{:S(2)}, u32[]{:S(2)}) %collective-permute-start.16) | collective-permute-done | bytes 1048608 | tf_op jit(solution)/shard_map/ppermute | solution.py:102
  547.4 20.2 %collective-permute-done.18 = bf16[1024,512]{1,0:T(8,128)(2,1)S(1)} collective-permute-done((bf16[1024,512]{1,0:T(8,128)(2,1)S(1)}, bf16[1024,512]{1,0:T(8,128)(2,1)S(1)}, u32[]{:S(2)}, u32[]{:S(2)}) %collective-permute-start.18) | collective-permute-done | bytes 1048608 | tf_op jit(solution)/shard_map/ppermute | solution.py:102
  569.7 20.3 %collective-permute-done.20 = bf16[1024,512]{1,0:T(8,128)(2,1)S(1)} collective-permute-done((bf16[1024,512]{1,0:T(8,128)(2,1)S(1)}, bf16[1024,512]{1,0:T(8,128)(2,1)S(1)}, u32[]{:S(2)}, u32[]{:S(2)}) %collective-permute-start.20) | collective-permute-done | bytes 1048608 | tf_op jit(solution)/shard_map/ppermute | solution.py:102
  634.5 113.4 %collective-permute-done.21 = bf16[768,4096]{1,0:T(8,128)(2,1)} collective-permute-done((bf16[768,4096]{1,0:T(8,128)(2,1)S(1)}, bf16[768,4096]{1,0:T(8,128)(2,1)}, u32[]{:S(2)}, u32[]{:S(2)}) %collective-permute-start.21) | collective-permute-done | bytes 6291488 | tf_op jit(solution)/shard_map/ppermute | solution.py:123
  748.6 41.2 %fusion.8 = f32[1024,4096]{1,0:T(8,128)} fusion(bf16[1024,4096]{1,0:T(8,128)(2,1)S(1)} %bitcast.29, bf16[4096,4096]{1,0:T(8,128)(2,1)} %slice_dynamic-update-slice_fusion.9), kind=kOutput, calls=%fused_computation.91 | convolution fusion | flops 34359738368 | bytes 58720256 | tf_op jit(solution)/shard_map/dot_general | solution.py:201
  818.2 45.5 %add_convert_fusion = bf16[1024,4096]{1,0:T(8,128)(2,1)} fusion(f32[1024,4096]{1,0:T(8,128)} %fusion.8, bf16[1024,4096]{1,0:T(8,128)(2,1)} %param.8, bf16[1024,4096]{1,0:T(8,128)(2,1)} %constant_dynamic-update-slice_fusion.4, bf16[4096,4096]{1,0:T(8,128)(2,1)} %slice_dynamic-update-slice_fusion), kind=kOutput, calls=%fused_computation | convolution fusion | flops 34376515584 | bytes 75497472 | tf_op jit(solution)/shard_map/dot_general | solution.py:201
  (145 shorter events, 170.6 us)
Async XLA Ops:
  6.5 164.0 %all-gather.3.cloned.1.call-start = ((), (), s32[]{:S(2)}) async-start(), calls=%async_computation | async-start | bytes 10485760 | tf_op jit(solution)/shard_map/all_gather | solution.py:176
  21.5 577.3 %all-gather.5.cloned.1.call-start = ((), (), s32[]{:S(2)}) async-start(), calls=%async_computation.1 | async-start | bytes 10485760 | tf_op jit(solution)/shard_map/all_gather | solution.py:188
  28.5 70.4 %collective-permute-start = (bf16[2048,512]{1,0:T(8,128)(2,1)}, bf16[2048,512]{1,0:T(8,128)(2,1)}, u32[]{:S(2)}, u32[]{:S(2)}) collective-permute-start(bf16[2048,512]{1,0:T(8,128)(2,1)} %get-tuple-element.31), channel_id=1, source_target_pairs={{0,4},{4,0},{1,5},{5,1},{2,6},{6,2},{3,7},{7,3},{8,12},{12,8},{9,1... | collective-permute-start | bytes 6291464 | tf_op jit(solution)/shard_map/ppermute | solution.py:102
  40.4 46.1 %collective-permute-start.1 = (bf16[2048,128]{0,1:T(8,128)(2,1)}, bf16[2048,128]{0,1:T(8,128)(2,1)}, u32[]{:S(2)}, u32[]{:S(2)}) collective-permute-start(bf16[2048,128]{0,1:T(8,128)(2,1)} %bitcast.33), channel_id=1, source_target_pairs={{0,4},{4,0},{1,5},{5,1},{2,6},{6,2},{3,7},{7,3},{8,12},{12,8},{9,1... | collective-permute-start | bytes 1572872 | tf_op jit(solution)/shard_map/ppermute | solution.py:102
  43.4 54.3 %collective-permute-start.2 = (bf16[2048,128]{0,1:T(8,128)(2,1)}, bf16[2048,128]{0,1:T(8,128)(2,1)}, u32[]{:S(2)}, u32[]{:S(2)}) collective-permute-start(bf16[2048,128]{0,1:T(8,128)(2,1)} %bitcast.32), channel_id=1, source_target_pairs={{0,4},{4,0},{1,5},{5,1},{2,6},{6,2},{3,7},{7,3},{8,12},{12,8},{9,1... | collective-permute-start | bytes 1572872 | tf_op jit(solution)/shard_map/ppermute | solution.py:102
  95.3 105.2 %collective-permute-start.13 = (bf16[2048,512]{1,0:T(8,128)(2,1)}, bf16[2048,512]{1,0:T(8,128)(2,1)}, u32[]{:S(2)}, u32[]{:S(2)}) collective-permute-start(bf16[2048,512]{1,0:T(8,128)(2,1)} %get-tuple-element.33), channel_id=1, source_target_pairs={{0,4},{4,0},{1,5},{5,1},{2,6},{6,2},{3,7},{7,3},{8,12},{12,8},{9,1... | collective-permute-start | bytes 6291464 | tf_op jit(solution)/shard_map/ppermute | solution.py:102
  195.3 92.2 %collective-permute-start.3 = (bf16[1024,512]{1,0:T(8,128)(2,1)}, bf16[1024,512]{1,0:T(8,128)(2,1)}, u32[]{:S(2)}, u32[]{:S(2)}) collective-permute-start(bf16[1024,512]{1,0:T(8,128)(2,1)} %get-tuple-element.39), channel_id=1, source_target_pairs={{0,4},{4,0},{1,5},{5,1},{2,6},{6,2},{3,7},{7,3},{8,12},{12,8},{9,1... | collective-permute-start | bytes 3145736 | tf_op jit(solution)/shard_map/ppermute | solution.py:102
  195.6 93.2 %collective-permute-start.4 = (bf16[1024,512]{1,0:T(8,128)(2,1)}, bf16[1024,512]{1,0:T(8,128)(2,1)}, u32[]{:S(2)}, u32[]{:S(2)}) collective-permute-start(bf16[1024,512]{1,0:T(8,128)(2,1)} %get-tuple-element.37), channel_id=1, source_target_pairs={{0,1},{1,2},{2,3},{3,0},{4,5},{5,6},{6,7},{7,4},{8,9},{9,10},{10,1... | collective-permute-start | bytes 3145736 | tf_op jit(solution)/shard_map/ppermute | solution.py:102
  195.6 123.0 %collective-permute-start.6 = (bf16[1024,512]{1,0:T(8,128)(2,1)}, bf16[1024,512]{1,0:T(8,128)(2,1)}, u32[]{:S(2)}, u32[]{:S(2)}) collective-permute-start(bf16[1024,512]{1,0:T(8,128)(2,1)} %get-tuple-element.36), channel_id=1, source_target_pairs={{0,2},{1,3},{2,0},{3,1},{4,6},{5,7},{6,4},{7,5},{8,10},{9,11},{10,... | collective-permute-start | bytes 3145736 | tf_op jit(solution)/shard_map/ppermute | solution.py:102
  198.0 238.6 %collective-permute-start.8 = (bf16[1024,512]{1,0:T(8,128)(2,1)}, bf16[1024,512]{1,0:T(8,128)(2,1)S(1)}, u32[]{:S(2)}, u32[]{:S(2)}) collective-permute-start(bf16[1024,512]{1,0:T(8,128)(2,1)} %get-tuple-element.35), channel_id=1, source_target_pairs={{0,3},{1,0},{2,1},{3,2},{4,7},{5,4},{6,5},{7,6},{8,11},{9,8},{10,9... | collective-permute-start | bytes 3145736 | tf_op jit(solution)/shard_map/ppermute | solution.py:102
  219.9 371.3 %collective-permute-start.10 = (bf16[768,4096]{1,0:T(8,128)(2,1)}, bf16[768,4096]{1,0:T(8,128)(2,1)}, u32[]{:S(2)}, u32[]{:S(2)}) collective-permute-start(bf16[768,4096]{1,0:T(8,128)(2,1)} %pad_maximum_fusion), channel_id=1, source_target_pairs={{0,16},{8,24},{16,0},{24,8},{1,17},{9,25},{17,1},{25,9},{2,18},{10... | collective-permute-start | bytes 18874376 | tf_op jit(solution)/shard_map/ppermute | solution.py:123
  287.5 151.4 %collective-permute-start.14 = (bf16[1024,512]{1,0:T(8,128)(2,1)S(1)}, bf16[1024,512]{1,0:T(8,128)(2,1)S(1)}, u32[]{:S(2)}, u32[]{:S(2)}) collective-permute-start(bf16[1024,512]{1,0:T(8,128)(2,1)S(1)} %get-tuple-element.44), channel_id=1, source_target_pairs={{0,4},{4,0},{1,5},{5,1},{2,6},{6,2},{3,7},{7,3},{8,12},{12,8},{9,1... | collective-permute-start | bytes 3145736 | tf_op jit(solution)/shard_map/ppermute | solution.py:102
  288.7 187.0 %collective-permute-start.15 = (bf16[1024,512]{1,0:T(8,128)(2,1)S(1)}, bf16[1024,512]{1,0:T(8,128)(2,1)S(1)}, u32[]{:S(2)}, u32[]{:S(2)}) collective-permute-start(bf16[1024,512]{1,0:T(8,128)(2,1)S(1)} %get-tuple-element.42), channel_id=1, source_target_pairs={{0,1},{1,2},{2,3},{3,0},{4,5},{5,6},{6,7},{7,4},{8,9},{9,10},{10,1... | collective-permute-start | bytes 3145736 | tf_op jit(solution)/shard_map/ppermute | solution.py:102
  318.6 157.2 %collective-permute-start.17 = (bf16[1024,512]{1,0:T(8,128)(2,1)S(1)}, bf16[1024,512]{1,0:T(8,128)(2,1)S(1)}, u32[]{:S(2)}, u32[]{:S(2)}) collective-permute-start(bf16[1024,512]{1,0:T(8,128)(2,1)S(1)} %get-tuple-element.41), channel_id=1, source_target_pairs={{0,2},{1,3},{2,0},{3,1},{4,6},{5,7},{6,4},{7,5},{8,10},{9,11},{10,... | collective-permute-start | bytes 3145736 | tf_op jit(solution)/shard_map/ppermute | solution.py:102
  436.6 61.8 %collective-permute-start.19 = (bf16[1024,512]{1,0:T(8,128)(2,1)}, bf16[1024,512]{1,0:T(8,128)(2,1)S(1)}, u32[]{:S(2)}, u32[]{:S(2)}) collective-permute-start(bf16[1024,512]{1,0:T(8,128)(2,1)} %get-tuple-element.40), channel_id=1, source_target_pairs={{0,3},{1,0},{2,1},{3,2},{4,7},{5,4},{6,5},{7,6},{8,11},{9,8},{10,9... | collective-permute-start | bytes 3145736 | tf_op jit(solution)/shard_map/ppermute | solution.py:102
  438.9 65.1 %collective-permute-start.5 = (bf16[1024,512]{1,0:T(8,128)(2,1)}, bf16[1024,512]{1,0:T(8,128)(2,1)}, u32[]{:S(2)}, u32[]{:S(2)}) collective-permute-start(bf16[1024,512]{1,0:T(8,128)(2,1)} %collective-permute-done.4), channel_id=1, source_target_pairs={{0,4},{4,0},{1,5},{5,1},{2,6},{6,2},{3,7},{7,3},{8,12},{12,8},{9,1... | collective-permute-start | bytes 3145736 | tf_op jit(solution)/shard_map/ppermute | solution.py:102
  476.7 46.0 %collective-permute-start.9 = (bf16[1024,512]{1,0:T(8,128)(2,1)S(1)}, bf16[1024,512]{1,0:T(8,128)(2,1)}, u32[]{:S(2)}, u32[]{:S(2)}) collective-permute-start(bf16[1024,512]{1,0:T(8,128)(2,1)S(1)} %collective-permute-done.8), channel_id=1, source_target_pairs={{0,4},{4,0},{1,5},{5,1},{2,6},{6,2},{3,7},{7,3},{8,12},{12,8},{9,1... | collective-permute-start | bytes 3145736 | tf_op jit(solution)/shard_map/ppermute | solution.py:102
  498.3 46.8 %collective-permute-start.16 = (bf16[1024,512]{1,0:T(8,128)(2,1)}, bf16[1024,512]{1,0:T(8,128)(2,1)S(1)}, u32[]{:S(2)}, u32[]{:S(2)}) collective-permute-start(bf16[1024,512]{1,0:T(8,128)(2,1)} %copy-done.4), channel_id=1, source_target_pairs={{0,4},{4,0},{1,5},{5,1},{2,6},{6,2},{3,7},{7,3},{8,12},{12,8},{9,1... | collective-permute-start | bytes 3145736 | tf_op jit(solution)/shard_map/ppermute | solution.py:102
  503.9 63.7 %collective-permute-start.18 = (bf16[1024,512]{1,0:T(8,128)(2,1)S(1)}, bf16[1024,512]{1,0:T(8,128)(2,1)S(1)}, u32[]{:S(2)}, u32[]{:S(2)}) collective-permute-start(bf16[1024,512]{1,0:T(8,128)(2,1)S(1)} %collective-permute-done.17), channel_id=1, source_target_pairs={{0,4},{4,0},{1,5},{5,1},{2,6},{6,2},{3,7},{7,3},{8,12},{12,8},{9,1... | collective-permute-start | bytes 3145736 | tf_op jit(solution)/shard_map/ppermute | solution.py:102
  509.1 80.9 %collective-permute-start.20 = (bf16[1024,512]{1,0:T(8,128)(2,1)S(1)}, bf16[1024,512]{1,0:T(8,128)(2,1)S(1)}, u32[]{:S(2)}, u32[]{:S(2)}) collective-permute-start(bf16[1024,512]{1,0:T(8,128)(2,1)S(1)} %collective-permute-done.19), channel_id=1, source_target_pairs={{0,4},{4,0},{1,5},{5,1},{2,6},{6,2},{3,7},{7,3},{8,12},{12,8},{9,1... | collective-permute-start | bytes 3145736 | tf_op jit(solution)/shard_map/ppermute | solution.py:102
  522.7 92.1 %collective-permute-start.11 = (bf16[768,4096]{1,0:T(8,128)(2,1)}, bf16[768,4096]{1,0:T(8,128)(2,1)}, u32[]{:S(2)}, u32[]{:S(2)}) collective-permute-start(bf16[768,4096]{1,0:T(8,128)(2,1)} %pad_maximum_fusion), channel_id=1, source_target_pairs={{0,8},{8,0},{16,24},{24,16},{1,9},{9,1},{17,25},{25,17},{2,10},{10... | collective-permute-start | bytes 18874376 | tf_op jit(solution)/shard_map/ppermute | solution.py:123
  610.5 137.3 %collective-permute-start.21 = (bf16[768,4096]{1,0:T(8,128)(2,1)S(1)}, bf16[768,4096]{1,0:T(8,128)(2,1)}, u32[]{:S(2)}, u32[]{:S(2)}) collective-permute-start(bf16[768,4096]{1,0:T(8,128)(2,1)S(1)} %pad_maximum_fusion.1), channel_id=1, source_target_pairs={{0,16},{8,24},{16,0},{24,8},{1,17},{9,25},{17,1},{25,9},{2,18},{10... | collective-permute-start | bytes 18874376 | tf_op jit(solution)/shard_map/ppermute | solution.py:123
  624.4 174.8 %collective-permute-start.22 = (bf16[768,4096]{1,0:T(8,128)(2,1)S(1)}, bf16[768,4096]{1,0:T(8,128)(2,1)}, u32[]{:S(2)}, u32[]{:S(2)}) collective-permute-start(bf16[768,4096]{1,0:T(8,128)(2,1)S(1)} %pad_maximum_fusion.1), channel_id=1, source_target_pairs={{0,8},{8,0},{16,24},{24,16},{1,9},{9,1},{17,25},{25,17},{2,10},{10... | collective-permute-start | bytes 18874376 | tf_op jit(solution)/shard_map/ppermute | solution.py:123
  747.9 60.8 %collective-permute-start.23 = (bf16[768,4096]{1,0:T(8,128)(2,1)}, bf16[768,4096]{1,0:T(8,128)(2,1)}, u32[]{:S(2)}, u32[]{:S(2)}) collective-permute-start(bf16[768,4096]{1,0:T(8,128)(2,1)} %collective-permute-done.21), channel_id=1, source_target_pairs={{0,8},{8,0},{16,24},{24,16},{1,9},{9,1},{17,25},{25,17},{2,10},{10... | collective-permute-start | bytes 18874376 | tf_op jit(solution)/shard_map/ppermute | solution.py:123
  (13 other events, 413.4 us)
Sparse Core Ops, SparseCore 0:
  21.6 148.8 all-gather.2
  172.1 298.0 all-gather.4
